TPU v7x, 32 devices: a whole 2x2x4 slice. The times are simulated.
32 devices in a mesh: groups: 2 (over y), expert: 8 (over z, core), dp: 2 (over x).
Axes of the slice: x: 2, y: 2, z: 4, core: 2. Of those that a mesh axis runs over, the one named last changes fastest.
Arguments:
- tokens: bfloat16 [4096, 2048], P(('groups', 'expert', 'dp')), parts along dimension 0, may hold values from -6 to 6
- out_grads: bfloat16 [4096, 2048], P(('groups', 'expert', 'dp')), parts along dimension 0, may hold values from -3 to 3
- routes: int32 [4096, 8], P(('groups', 'expert', 'dp')), parts along dimension 0, may hold values from 0 to 15, all different within a row; in each aligned block of 128 rows (0 to 127, 128 to 255, ...) at most 72 rows name the same one
- gates: bfloat16 [4096, 8], P(('groups', 'expert', 'dp')), parts along dimension 0, may hold values from 0.049804688 to 0.5
- gate_weight: bfloat16 [16, 2048, 384], P('expert'), may hold values from -0.125 to 0.125
- up_weight: bfloat16 [16, 2048, 384], P('expert'), may hold values from -0.125 to 0.125
- down_weight: bfloat16 [16, 384, 2048], P('expert'), may hold values from -0.3125 to 0.3125
Outputs:
- input_grads: bfloat16 [4096, 2048], P(('groups', 'expert', 'dp')), parts along dimension 0
- gate_grads: bfloat16 [4096, 8], P(('groups', 'expert', 'dp')), parts along dimension 0
- gate_weight_grads: bfloat16 [32, 2048, 384], P(('groups', 'expert'), 'dp'), parts along dimension 0
- up_weight_grads: bfloat16 [32, 2048, 384], P(('groups', 'expert'), 'dp'), parts along dimension 0
- down_weight_grads: bfloat16 [32, 384, 2048], P(('groups', 'expert'), None, 'dp'), parts along dimension 0
There are 2 independent parts, one for each index of `groups`. A program takes and returns all parts, laid end to end along the dimension named above; an argument that names none is the same for every part. Nothing has to cross between parts.
Inputs may be any that keep to these rules, and one draw needn't show every extreme that they name: `routes`: each row names 8 different experts; among the rows of one device no expert is named more than 72 times, and in every draw some expert is named exactly 72 times by the rows of some device.
All inputs are finite; a program needn't handle non-finite values.
Results may differ from a plain program's by a relative error of at most 0.012.
Values may be sent and summed in bfloat16 or wider, within the bound.
A program may use at most 128 MiB of HBM per device.

v0:
```python
import jax
import jax.numpy as jnp
from jax import lax
from jax.sharding import PartitionSpec as P


def project_in(rows_x, gate_weight, up_weight):
    pre_gate = jnp.einsum("slcd,ldf->slcf", rows_x, gate_weight, preferred_element_type=jnp.float32)
    pre_up = jnp.einsum("slcd,ldf->slcf", rows_x, up_weight, preferred_element_type=jnp.float32)
    return (pre_gate, pre_up)


def per_device(tokens, out_grads, routes, gates, gate_weight, up_weight, down_weight):
    tok_rows, feature_width = tokens.shape
    top_count = routes.shape[1]
    local_experts = gate_weight.shape[0]
    group_count = lax.axis_size("expert")
    expert_count = local_experts * group_count
    capacity = min(
        tok_rows, max(2, (tok_rows * top_count * 9 + expert_count * 8 - 1) // (expert_count * 8))
    )
    flat_routes = routes.reshape(-1)
    onehot = (flat_routes[:, None] == jnp.arange(expert_count, dtype=jnp.int32)[None, :]).astype(
        jnp.int32
    )
    positions = jnp.sum((jnp.cumsum(onehot, axis=0) - 1) * onehot, axis=1)
    slot_index = flat_routes * capacity + positions
    sentinel = tok_rows * top_count
    slot_table = (
        jnp.full((expert_count * capacity,), sentinel, jnp.int32)
        .at[slot_index]
        .set(jnp.arange(sentinel, dtype=jnp.int32))
    )
    owners = slot_table // top_count
    padded_x = jnp.concatenate([tokens, jnp.zeros((1, feature_width), tokens.dtype)], axis=0)
    padded_dy = jnp.concatenate([out_grads, jnp.zeros((1, feature_width), out_grads.dtype)], axis=0)
    padded_gate = jnp.concatenate([gates.reshape(-1), jnp.zeros((1,), gates.dtype)], axis=0)
    shape_rows = (group_count, local_experts * capacity, feature_width)
    block_shape = (group_count, local_experts, capacity, feature_width)
    send_x = jnp.take(padded_x, owners, axis=0).reshape(shape_rows)
    send_dy = jnp.take(padded_dy, owners, axis=0).reshape(shape_rows)
    send_gate = jnp.take(padded_gate, slot_table).reshape(group_count, local_experts * capacity)
    recv_x, recv_dy, recv_gate = (
        lax.all_to_all(send_x, "expert", split_axis=0, concat_axis=0, tiled=True),
        lax.all_to_all(send_dy, "expert", split_axis=0, concat_axis=0, tiled=True),
        lax.all_to_all(send_gate, "expert", split_axis=0, concat_axis=0, tiled=True),
    )
    pre_gate, pre_up = project_in(recv_x.reshape(block_shape), gate_weight, up_weight)
    rows_x = recv_x.reshape(block_shape)
    rows_dy = recv_dy.reshape(block_shape)
    gate_col = recv_gate.reshape(group_count, local_experts, capacity, 1).astype(jnp.float32)
    sigmoid_gate = jax.nn.sigmoid(pre_gate)
    activated = pre_gate * sigmoid_gate
    hidden = activated * pre_up
    gated_hidden = (gate_col * hidden).astype(jnp.bfloat16)
    back_raw = jnp.einsum(
        "slcd,lfd->slcf", rows_dy, down_weight, preferred_element_type=jnp.float32
    )
    route_grad = jnp.sum(hidden * back_raw, axis=-1).astype(jnp.bfloat16)
    back = gate_col * back_raw
    grad_gate = (back * pre_up * sigmoid_gate * (1.0 + pre_gate * (1.0 - sigmoid_gate))).astype(
        jnp.bfloat16
    )
    grad_up = (back * activated).astype(jnp.bfloat16)
    down_part = jnp.einsum(
        "slcf,slcd->lfd", gated_hidden, rows_dy, preferred_element_type=jnp.float32
    ).astype(jnp.bfloat16)
    row_grads = (
        jnp.einsum("slcf,ldf->slcd", grad_gate, gate_weight, preferred_element_type=jnp.float32)
        + jnp.einsum("slcf,ldf->slcd", grad_up, up_weight, preferred_element_type=jnp.float32)
    ).astype(jnp.bfloat16)
    back_rows, back_route = (
        lax.all_to_all(
            row_grads.reshape(shape_rows), "expert", split_axis=0, concat_axis=0, tiled=True
        ),
        lax.all_to_all(
            route_grad.reshape(group_count, local_experts * capacity),
            "expert",
            split_axis=0,
            concat_axis=0,
            tiled=True,
        ),
    )
    picked = jnp.take(back_rows.reshape(expert_count * capacity, feature_width), slot_index, axis=0)
    picked = picked.reshape(tok_rows, top_count, feature_width)
    input_grads = jnp.sum(picked, axis=1, dtype=jnp.float32).astype(jnp.bfloat16)
    gate_grads = jnp.take(back_route.reshape(-1), slot_index).reshape(tok_rows, top_count)
    gate_part = jnp.einsum(
        "slcd,slcf->ldf", rows_x, grad_gate, preferred_element_type=jnp.float32
    ).astype(jnp.bfloat16)
    up_part = jnp.einsum(
        "slcd,slcf->ldf", rows_x, grad_up, preferred_element_type=jnp.float32
    ).astype(jnp.bfloat16)
    gate_sum, up_sum, down_sum = (
        lax.psum_scatter(gate_part, "dp", scatter_dimension=1, tiled=True).astype(jnp.float32),
        lax.psum_scatter(up_part, "dp", scatter_dimension=1, tiled=True).astype(jnp.float32),
        lax.psum_scatter(down_part, "dp", scatter_dimension=2, tiled=True).astype(jnp.float32),
    )
    return (
        input_grads,
        gate_grads,
        gate_sum.astype(jnp.bfloat16),
        up_sum.astype(jnp.bfloat16),
        down_sum.astype(jnp.bfloat16),
    )


def solution(mesh):
    in_specs = (
        P(("groups", "expert", "dp"), None),
        P(("groups", "expert", "dp"), None),
        P(("groups", "expert", "dp"), None),
        P(("groups", "expert", "dp"), None),
        P("expert", None, None),
        P("expert", None, None),
        P("expert", None, None),
    )
    out_specs = (
        P(("groups", "expert", "dp"), None),
        P(("groups", "expert", "dp"), None),
        P(("groups", "expert"), "dp", None),
        P(("groups", "expert"), "dp", None),
        P(("groups", "expert"), None, "dp"),
    )
    return jax.shard_map(
        per_device, mesh=mesh, in_specs=in_specs, out_specs=out_specs, check_vma=False
    )
```

profile of v0, /device:TPU:0, one launch (start us, length us, event | category | flops | bytes accessed | tf_op | source)
XLA Modules:
  0.0 462.9 jit_solution(1576886883880407843)
XLA Ops:
  7.2 0.0 copy-start
  7.2 0.9 copy.46
  8.1 0.1 eq.26
  8.2 0.1 reshape.163
  8.3 0.8 copy.51
  9.1 0.1 reshape.165
  9.2 4.5 reduce-window.6
  13.8 0.1 slice.18
  13.8 0.1 copy.49
  14.0 0.1 copy.50
  14.1 0.1 add_add_fusion
  14.2 0.1 mul.64
  14.3 4.3 scatter_custom_fusion
  18.7 7.3 %gather_fusion = bf16[1152]{0:T(1024)(128)(2,1)S(1)} fusion(bf16[1025]{0:T(1024)(128)(2,1)S(1)} %pad_maximum_fusion, s32[2048]{0:T(1024)S(1)} %pad_clamp_fusion.1), kind=kCustom, calls=%fused_computation.2 | custom fusion | bytes 9216 | tf_op jit(solution)/shard_map/jit(_take)/gather | solution.py:42
  26.0 0.7 select_n.75
  26.7 6.3 %all-to-all-start = ((bf16[8,1,144]{2,1,0:T(2,128)(2,1)}), bf16[8,1,144]{2,1,0:T(2,128)(2,1)S(1)}, u32[]{:S(2)}, u32[]{:S(2)}) async-start(bf16[8,1,144]{2,1,0:T(2,128)(2,1)} %select_n.75), calls=%async_computation | async-start | bytes 16384 | tf_op jit(solution)/shard_map/all_to_all | solution.py:46
  33.0 1.9 concatenate.11
  34.9 1.9 concatenate.10
  36.8 11.9 %gather_fusion.3 = bf16[1152,2048]{1,0:T(8,128)(2,1)} fusion(bf16[129,2048]{1,0:T(8,128)(2,1)} %concatenate.10, s32[2048]{0:T(1024)S(1)} %pad_clamp_fusion), kind=kCustom, calls=%fused_computation.clone | custom fusion | bytes 9441792 | tf_op jit(solution)/shard_map/jit(_take)/gather | solution.py:41
  48.7 11.8 %gather_fusion.4 = bf16[1152,2048]{1,0:T(8,128)(2,1)} fusion(bf16[129,2048]{1,0:T(8,128)(2,1)} %concatenate.11, s32[2048]{0:T(1024)S(1)} %pad_clamp_fusion), kind=kCustom, calls=%fused_computation.1.clone | custom fusion | bytes 9441792 | tf_op jit(solution)/shard_map/jit(_take)/gather | solution.py:40
  60.5 8.7 %broadcast_select_fusion.1 = (bf16[1152,2048]{1,0:T(8,128)(2,1)}, bf16[1152,2048]{1,0:T(8,128)(2,1)}) fusion(bf16[1152,2048]{1,0:T(8,128)(2,1)} %gather_fusion.3, pred[1152]{0:T(1024)(128)(4,1)S(1)} %get-tuple-element.23, bf16[1152,2048]{1,0:T(8,128)(2,1)} %gather_fusion.4), kind=kLoop, calls=%fused_computation.12 | loop fusion | flops 4718592 | bytes 18875520 | tf_op jit(solution)/shard_map/jit(_take)/select_n | solution.py:41
  69.1 0.0 all-to-all-done
  69.1 110.5 %all_to_all.27 = bf16[8,144,2048]{2,1,0:T(8,128)(2,1)} all-to-all(bf16[8,144,2048]{2,1,0:T(8,128)(2,1)} %bitcast.110), channel_id=1, replica_groups=mesh['groups'=2,'expert'=8,'dp'=2] {'expert'}, dimensions={0} | all-to-all | bytes 9437184 | tf_op jit(solution)/shard_map/all_to_all | solution.py:44
  179.7 4.6 all-to-all-start.1
  184.3 0.2 reduce-scatter.8.cloned.1.call-start
  184.5 0.1 reshape.173
  184.6 0.0 copy-done
  184.6 0.0 copy-start.1
  184.6 0.0 copy-start.2
  184.6 6.3 %fusion.2 = f32[2,8,72,384]{3,2,1,0:T(8,128)} fusion(bf16[8,2,72,2048]{3,2,1,0:T(8,128)(2,1)} %bitcast.112, bf16[2,2048,384]{2,1,0:T(8,128)(2,1)S(1)} %copy-done), kind=kOutput, calls=%fused_computation.15 | convolution fusion | flops 1811939328 | bytes 9633792 | tf_op jit(solution)/shard_map/slcd,ldf->slcf/dot_general | solution.py:8
  190.9 0.0 copy-done.1
  190.9 0.0 copy-done.2
  190.9 3.8 fusion.4
  194.8 94.7 %all-to-all-done.1 = bf16[8,144,2048]{2,1,0:T(8,128)(2,1)} async-done(((bf16[8,144,2048]{2,1,0:T(8,128)(2,1)}), bf16[8,144,2048]{2,1,0:T(8,128)(2,1)}, u32[]{:S(2)}, u32[]{:S(2)}) %all-to-all-start.1) | async-done | bytes 4718624 | tf_op jit(solution)/shard_map/all_to_all | solution.py:45
  289.5 7.9 %bitcast_convert_fusion = bf16[2,384,2048]{2,1,0:T(8,128)(2,1)} fusion(bf16[8,2,72,2048]{3,2,1,0:T(8,128)(2,1)} %bitcast.5, f32[8,2,72]{2,0,1:T(8,128)S(1)} %copy.53, f32[2,8,72,384]{3,2,1,0:T(8,128)} %fusion.4, f32[2,8,72,384]{3,2,1,0:T(8,128)} %fusion.2), kind=kOutput, calls=%fused_computation.7 | convolution fusion | flops 1816608768 | bytes 11407872 | tf_op jit(solution)/shard_map/slcf,slcd->lfd/dot_general | solution.py:65
  297.4 0.0 reduce-scatter.8.cloned.1.call-update
  297.4 0.3 reduce-scatter.6.cloned.1.call-start
  297.7 8.4 %fusion.25 = (bf16[8,2,72]{2,0,1:T(8,128)(2,1)S(1)}, bf16[8,2,72,384]{3,2,0,1:T(8,128)(2,1)}, bf16[8,2,72,384]{3,2,0,1:T(8,128)(2,1)S(1)}) fusion(f32[2,8,72,384]{3,2,1,0:T(8,128)} %fusion.4, f32[2,8,72,384]{3,2,1,0:T(8,128)} %fusion.2, f32[8,2,72]{2,0,1:T(8,128)S(1)} %copy.53, bf16[2,384,2048]{2,1,0:T(8,128)(2,1)} %param.15, ...), kind=kOutput, calls=%fused_computation.43 | convolution fusion | flops 1819458432 | bytes 13179648 | tf_op jit(solution)/shard_map/slcd,lfd->slcf/dot_general | solution.py:56
  306.1 0.0 copy-start.4
  306.1 0.9 copy-done.4
  307.0 7.2 %bitcast_convert_fusion.1 = bf16[2,2048,384]{2,1,0:T(8,128)(2,1)} fusion(bf16[8,2,72,2048]{3,2,1,0:T(8,128)(2,1)} %bitcast.113, bf16[8,2,72,384]{3,2,0,1:T(8,128)(2,1)S(1)} %get-tuple-element.27), kind=kOutput, calls=%fused_computation.8 | convolution fusion | flops 1813512192 | bytes 8749056 | tf_op jit(solution)/shard_map/slcd,slcf->ldf/dot_general | solution.py:91
  314.2 0.0 reduce-scatter.6.cloned.1.call-update
  314.3 0.7 convert_element_type.76
  315.0 3.3 all-to-all-start.4
  318.3 0.0 copy-start.3
  318.3 4.0 fusion.12
  322.3 0.0 copy-done.3
  322.3 4.2 fusion
  326.5 2.6 copy.57
  329.1 0.0 all-to-all-done.4
  329.1 5.0 %all-to-all-start.3 = ((bf16[8,144,2048]{2,1,0:T(8,128)(2,1)}), bf16[8,144,2048]{2,1,0:T(8,128)(2,1)}, u32[]{:S(2)}, u32[]{:S(2)}) async-start(bf16[8,144,2048]{2,1,0:T(8,128)(2,1)} %bitcast.111), calls=%async_computation.3 | async-start | bytes 9437184 | tf_op jit(solution)/shard_map/all_to_all | solution.py:73
  334.1 0.3 reduce-scatter.4.cloned.1.call-start
  334.4 7.5 %bitcast_convert_fusion.2 = bf16[2,2048,384]{2,1,0:T(8,128)(2,1)} fusion(bf16[8,2,72,2048]{3,2,1,0:T(8,128)(2,1)} %bitcast.114, bf16[8,2,72,384]{3,2,0,1:T(8,128)(2,1)} %get-tuple-element.26), kind=kOutput, calls=%fused_computation.9 | convolution fusion | flops 1813512192 | bytes 8749056 | tf_op jit(solution)/shard_map/slcd,slcf->ldf/dot_general | solution.py:88
  341.9 0.0 reduce-scatter.4.cloned.1.call-update
  341.9 0.1 reduce_sum.35
  342.0 0.1 reshape.172
  342.1 6.8 %gather_fusion.2 = bf16[1024]{0:T(1024)(128)(2,1)S(1)} fusion(bf16[1152]{0:T(1024)(128)(2,1)S(1)} %reshape.172, s32[1024]{0:T(1024)S(1)} %broadcast_clamp_fusion), kind=kCustom, calls=%fused_computation.4 | custom fusion | bytes 8192 | tf_op jit(solution)/shard_map/jit(_take)/gather | solution.py:87
  349.0 0.1 gather.23
  349.1 0.7 copy.63
  349.7 89.7 %all-to-all-done.3 = bf16[8,144,2048]{2,1,0:T(8,128)(2,1)} async-done(((bf16[8,144,2048]{2,1,0:T(8,128)(2,1)}), bf16[8,144,2048]{2,1,0:T(8,128)(2,1)}, u32[]{:S(2)}, u32[]{:S(2)}) %all-to-all-start.3) | async-done | bytes 4718624 | tf_op jit(solution)/shard_map/all_to_all | solution.py:73
  439.5 11.8 %gather_fusion.1 = bf16[1024,2048]{1,0:T(8,128)(2,1)} fusion(bf16[1152,2048]{1,0:T(8,128)(2,1)} %bitcast.20, s32[1024]{0:T(1024)S(1)} %broadcast_clamp_fusion), kind=kCustom, calls=%fused_computation.3 | custom fusion | bytes 8392704 | tf_op jit(solution)/shard_map/jit(_take)/gather | solution.py:84
  451.2 5.1 %fusion.1 = bf16[128,2048]{1,0:T(8,128)(2,1)} fusion(bf16[1024,2048]{1,0:T(8,128)(2,1)} %gather_fusion.1, pred[128,8]{1,0:T(8,128)(4,1)S(1)} %get-tuple-element.22), kind=kLoop, calls=%fused_computation.14 | loop fusion | flops 3932160 | bytes 4719616 | tf_op jit(solution)/shard_map/reduce_sum | solution.py:86
  456.4 0.0 reduce-scatter.8.cloned.1.call-done
  456.4 0.0 reduce-scatter.6.cloned.1.call-done
  (20 shorter events, 0.2 us)
Async XLA Ops:
  7.2 177.5 %copy-start = (bf16[2,2048,384]{2,1,0:T(8,128)(2,1)S(1)}, bf16[2,2048,384]{2,1,0:T(8,128)(2,1)}, u32[]{:S(2)}) copy-start(bf16[2,2048,384]{2,1,0:T(8,128)(2,1)} %param.13) | copy-start | bytes 9437188
  26.7 42.5 %all-to-all-start = ((bf16[8,1,144]{2,1,0:T(2,128)(2,1)}), bf16[8,1,144]{2,1,0:T(2,128)(2,1)S(1)}, u32[]{:S(2)}, u32[]{:S(2)}) async-start(bf16[8,1,144]{2,1,0:T(2,128)(2,1)} %select_n.75), calls=%async_computation | async-start | bytes 16384 | tf_op jit(solution)/shard_map/all_to_all | solution.py:46
  179.7 109.9 %all-to-all-start.1 = ((bf16[8,144,2048]{2,1,0:T(8,128)(2,1)}), bf16[8,144,2048]{2,1,0:T(8,128)(2,1)}, u32[]{:S(2)}, u32[]{:S(2)}) async-start(bf16[8,144,2048]{2,1,0:T(8,128)(2,1)} %bitcast.109), calls=%async_computation.1 | async-start | bytes 9437184 | tf_op jit(solution)/shard_map/all_to_all | solution.py:45
  184.3 272.1 %reduce-scatter.8.cloned.1.call-start = ((), (), s32[]{:S(2)}) async-start(), calls=%async_computation.10 | async-start | bytes 4718592 | tf_op jit(solution)/shard_map/reduce_scatter | solution.py:97
  184.6 6.3 %copy-start.1 = (bf16[8,144,2048]{2,1,0:T(8,128)(2,1)S(1)}, bf16[8,144,2048]{2,1,0:T(8,128)(2,1)}, u32[]{:S(2)}) copy-start(bf16[8,144,2048]{2,1,0:T(8,128)(2,1)} %all_to_all.27) | copy-start | bytes 14155780
  184.6 6.3 %copy-start.2 = (bf16[2,2048,384]{2,1,0:T(8,128)(2,1)S(1)}, bf16[2,2048,384]{2,1,0:T(8,128)(2,1)}, u32[]{:S(2)}) copy-start(bf16[2,2048,384]{2,1,0:T(8,128)(2,1)} %param.14) | copy-start | bytes 9437188
  297.4 158.9 %reduce-scatter.6.cloned.1.call-start = ((), (), s32[]{:S(2)}) async-start(), calls=%async_computation.9 | async-start | bytes 4718592 | tf_op jit(solution)/shard_map/reduce_scatter | solution.py:96
  306.1 0.9 copy-start.4
  315.0 14.1 %all-to-all-start.4 = ((bf16[8,1,144]{2,1,0:T(2,128)(2,1)}), bf16[8,1,144]{2,1,0:T(2,128)(2,1)S(1)}, u32[]{:S(2)}, u32[]{:S(2)}) async-start(bf16[8,1,144]{2,1,0:T(2,128)(2,1)} %convert_element_type.76), calls=%async_computation.4 | async-start | bytes 16384 | tf_op jit(solution)/shard_map/all_to_all | solution.py:76
  318.3 4.0 copy-start.3
  329.1 110.4 %all-to-all-start.3 = ((bf16[8,144,2048]{2,1,0:T(8,128)(2,1)}), bf16[8,144,2048]{2,1,0:T(8,128)(2,1)}, u32[]{:S(2)}, u32[]{:S(2)}) async-start(bf16[8,144,2048]{2,1,0:T(8,128)(2,1)} %bitcast.111), calls=%async_computation.3 | async-start | bytes 9437184 | tf_op jit(solution)/shard_map/all_to_all | solution.py:73
  334.1 122.3 %reduce-scatter.4.cloned.1.call-start = ((), (), s32[]{:S(2)}) async-start(), calls=%async_computation.8 | async-start | bytes 4718592 | tf_op jit(solution)/shard_map/reduce_scatter | solution.py:95
Sparse Core Ops, SparseCore 0:
  297.5 42.2 reduce-scatter.7
  342.7 43.3 reduce-scatter.5
  388.9 43.3 reduce-scatter.3
where the time goes:
time: 464 us; the launch traced here: 463 us
  waiting for transfers between devices  184 us (40%)
  blocking collectives  111 us (24%)
  local copies, waits for them, and re-layouts  65.9 us (14%)
  matrix products  49.3 us (11%)
  starting transfers between devices  20.1 us (4%)
  other arithmetic  18.7 us (4%)
  between operations  14 us (3%)
    all_to_all x1, blocking collectives, per_device(): lax.all_to_all(send_x, 'expert', split_axis=0, concat_axis=0, tiled=True)  111 us
    all_to_all x1, waiting for transfers between devices, per_device(): lax.all_to_all(send_dy, 'expert', split_axis=0, concat_axis=0, tiled=True)  94.7 us
    all_to_all x1, waiting for transfers between devices, per_device(): lax.all_to_all(row_grads.reshape(shape_rows), 'expert', split_axis=0, con...  89.7 us
    gather x1, local copies, waits for them, and re-layouts, per_device(): send_dy = jnp.take(padded_dy, owners, axis=0).reshape(shape_rows)  11.9 us
    gather x1, local copies, waits for them, and re-layouts, per_device(): jnp.take(back_rows.reshape(expert_count * capacity, feature_width), slot_...  11.8 us
    gather x1, local copies, waits for them, and re-layouts, per_device(): send_x = jnp.take(padded_x, owners, axis=0).reshape(shape_rows)  11.8 us
  transfers between devices with their start and end apart: 7, of which 2 were waited for; matrix products, arithmetic and copies ran while one was open for 23% of the time, Pallas kernels for 0%

commit v1 on v0

--- a/solution.py
+++ b/solution.py
@@ -2,6 +2,28 @@
 import jax.numpy as jnp
 from jax import lax
 from jax.sharding import PartitionSpec as P
+
+
+def cut_along(value, dim, size):
+    before, after = (value.shape[:dim], value.shape[dim + 1 :])
+    return jnp.moveaxis(value.reshape(*before, size, -1, *after), dim, 0)
+
+
+def laid_out(blocks, dim):
+    shape = list(blocks.shape[1:])
+    shape[dim] *= blocks.shape[0]
+    return jnp.moveaxis(blocks, 0, dim).reshape(shape)
+
+
+def exchange_in_pairs(value, axis, split_dim, concat_dim):
+    size, index = (lax.axis_size(axis), lax.axis_index(axis))
+    blocks = cut_along(value, split_dim, size)
+    gathered = [blocks[index]]
+    for step in range(1, size):
+        sent = blocks[index ^ step]
+        gathered.append(lax.ppermute(sent, axis, [(i, i ^ step) for i in range(size)]))
+    blocks = jnp.stack(gathered)[index ^ jnp.arange(size)]
+    return laid_out(blocks, concat_dim)
 
 
 def project_in(rows_x, gate_weight, up_weight):
@@ -70,9 +92,7 @@
         + jnp.einsum("slcf,ldf->slcd", grad_up, up_weight, preferred_element_type=jnp.float32)
     ).astype(jnp.bfloat16)
     back_rows, back_route = (
-        lax.all_to_all(
-            row_grads.reshape(shape_rows), "expert", split_axis=0, concat_axis=0, tiled=True
-        ),
+        exchange_in_pairs(row_grads.reshape(shape_rows), "expert", 0, 0),
         lax.all_to_all(
             route_grad.reshape(group_count, local_experts * capacity),
             "expert",

time: 464 us -> 480 us (1.034)
  local copies, waits for them, and re-layouts: 65.9 us -> 83.1 us
  waiting for transfers between devices: 184 us -> 179 us
    all_to_all x1 -> x0, waiting for transfers between devices: 89.7 us -> none  [per_device(): lax.all_to_all(row_grads.reshape(shape_rows), 'expert', split_axis=0, con...]
    ppermute x0 -> x7, waiting for transfers between devices: none -> 83.8 us  [exchange_in_pairs(): lax.ppermute(sent, axis, [(i, i ^ step) for i in range(size)])]
    unnamed x13 -> x19, local copies, waits for them, and re-layouts: 3.35 us -> 13.1 us
    ppermute x0 -> x7, starting transfers between devices: none -> 8.98 us  [exchange_in_pairs(): lax.ppermute(sent, axis, [(i, i ^ step) for i in range(size)])]
    gather x0 -> x1, local copies, waits for them, and re-layouts: none -> 5.34 us  [exchange_in_pairs(): blocks = jnp.stack(gathered)[index ^ jnp.arange(size)]]
    all_to_all x1 -> x0, starting transfers between devices: 5 us -> none  [per_device(): lax.all_to_all(row_grads.reshape(shape_rows), 'expert', split_axis=0, con...]
  transfers between devices with their start and end apart: 7 -> 13, of which waited for: 2 -> 4; matrix products, arithmetic and copies ran while one was open for 23% -> 26% of each run, Pallas kernels for 0% -> 0%
where the time goes in v1:
time: 480 us; the launch traced here: 479 us
  waiting for transfers between devices  179 us (37%)
  blocking collectives  111 us (23%)
  local copies, waits for them, and re-layouts  83.1 us (17%)
  matrix products  49.2 us (10%)
  starting transfers between devices  24.3 us (5%)
  other arithmetic  18.7 us (4%)
  between operations  14 us (3%)
    all_to_all x1, blocking collectives, per_device(): lax.all_to_all(send_x, 'expert', split_axis=0, concat_axis=0, tiled=True)  111 us
    all_to_all x1, waiting for transfers between devices, per_device(): lax.all_to_all(send_dy, 'expert', split_axis=0, concat_axis=0, tiled=True)  94.8 us
    ppermute x7, waiting for transfers between devices, exchange_in_pairs(): lax.ppermute(sent, axis, [(i, i ^ step) for i in range(size)])  83.8 us
    unnamed x19, local copies, waits for them, and re-layouts  13.1 us
    gather x1, local copies, waits for them, and re-layouts, per_device(): send_dy = jnp.take(padded_dy, owners, axis=0).reshape(shape_rows)  11.8 us
    gather x1, local copies, waits for them, and re-layouts, per_device(): send_x = jnp.take(padded_x, owners, axis=0).reshape(shape_rows)  11.8 us
    gather x1, local copies, waits for them, and re-layouts, per_device(): jnp.take(back_rows.reshape(expert_count * capacity, feature_width), slot_...  11.8 us
  transfers between devices with their start and end apart: 13, of which 4 were waited for; matrix products, arithmetic and copies ran while one was open for 26% of the time, Pallas kernels for 0%

profile of v1, /device:TPU:0, one launch (start us, length us, event | category | flops | bytes accessed | tf_op | source)
XLA Modules:
  0.0 478.5 jit_solution(13823452807296623011)
XLA Ops:
  7.2 0.9 copy.46
  8.1 0.1 eq.26
  8.2 0.1 reshape.173
  8.3 4.5 reduce-window.6
  12.9 0.1 slice.20
  12.9 0.1 copy.49
  13.1 0.1 copy.50
  13.2 0.1 add_add_fusion
  13.3 0.1 mul.64
  13.4 4.3 scatter_custom_fusion
  17.8 0.8 copy.51
  18.6 0.1 reshape.175
  18.7 7.3 %gather_fusion = bf16[1152]{0:T(1024)(128)(2,1)S(1)} fusion(bf16[1025]{0:T(1024)(128)(2,1)S(1)} %pad_maximum_fusion, s32[2048]{0:T(1024)S(1)} %get-tuple-element.39), kind=kCustom, calls=%fused_computation.2 | custom fusion | bytes 9216 | tf_op jit(solution)/shard_map/jit(_take)/gather | solution.py:64
  26.0 0.7 select_n.118
  26.7 6.3 %all-to-all-start = ((bf16[8,1,144]{2,1,0:T(2,128)(2,1)}), bf16[8,1,144]{2,1,0:T(2,128)(2,1)S(1)}, u32[]{:S(2)}, u32[]{:S(2)}) async-start(bf16[8,1,144]{2,1,0:T(2,128)(2,1)} %select_n.118), calls=%async_computation | async-start | bytes 16384 | tf_op jit(solution)/shard_map/all_to_all | solution.py:68
  33.0 1.9 concatenate.11
  34.9 1.9 concatenate.10
  36.8 11.8 %gather_fusion.4 = bf16[1152,2048]{1,0:T(8,128)(2,1)} fusion(bf16[129,2048]{1,0:T(8,128)(2,1)} %concatenate.10, s32[2048]{0:T(1024)S(1)} %get-tuple-element.38), kind=kCustom, calls=%fused_computation.clone | custom fusion | bytes 9441792 | tf_op jit(solution)/shard_map/jit(_take)/gather | solution.py:63
  48.7 11.8 %gather_fusion.5 = bf16[1152,2048]{1,0:T(8,128)(2,1)} fusion(bf16[129,2048]{1,0:T(8,128)(2,1)} %concatenate.11, s32[2048]{0:T(1024)S(1)} %get-tuple-element.38), kind=kCustom, calls=%fused_computation.1.clone | custom fusion | bytes 9441792 | tf_op jit(solution)/shard_map/jit(_take)/gather | solution.py:62
  60.4 8.7 %broadcast_select_fusion.1 = (bf16[1152,2048]{1,0:T(8,128)(2,1)}, bf16[1152,2048]{1,0:T(8,128)(2,1)}) fusion(bf16[1152,2048]{1,0:T(8,128)(2,1)} %gather_fusion.4, pred[1152]{0:T(1024)(128)(4,1)S(1)} %get-tuple-element.23, bf16[1152,2048]{1,0:T(8,128)(2,1)} %gather_fusion.5), kind=kLoop, calls=%fused_computation.13 | loop fusion | flops 4718592 | bytes 18875520 | tf_op jit(solution)/shard_map/jit(_take)/select_n | solution.py:63
  69.1 110.5 %all_to_all.22 = bf16[8,144,2048]{2,1,0:T(8,128)(2,1)} all-to-all(bf16[8,144,2048]{2,1,0:T(8,128)(2,1)} %bitcast.142), channel_id=1, replica_groups=mesh['groups'=2,'expert'=8,'dp'=2] {'expert'}, dimensions={0} | all-to-all | bytes 9437184 | tf_op jit(solution)/shard_map/all_to_all | solution.py:66
  179.6 4.6 all-to-all-start.1
  184.2 0.2 reduce-scatter.8.cloned.1.call-start
  184.5 0.1 reshape.181
  184.6 6.3 %fusion.2 = f32[2,8,72,384]{3,2,1,0:T(8,128)} fusion(bf16[8,2,72,2048]{3,2,1,0:T(8,128)(2,1)} %bitcast.145, bf16[2,2048,384]{2,1,0:T(8,128)(2,1)S(1)} %copy-done), kind=kOutput, calls=%fused_computation.16 | convolution fusion | flops 1811939328 | bytes 9633792 | tf_op jit(solution)/shard_map/slcd,ldf->slcf/dot_general | solution.py:30
  190.9 3.8 fusion.4
  194.7 94.8 %all-to-all-done.1 = bf16[8,144,2048]{2,1,0:T(8,128)(2,1)} async-done(((bf16[8,144,2048]{2,1,0:T(8,128)(2,1)}), bf16[8,144,2048]{2,1,0:T(8,128)(2,1)}, u32[]{:S(2)}, u32[]{:S(2)}) %all-to-all-start.1) | async-done | bytes 4718624 | tf_op jit(solution)/shard_map/all_to_all | solution.py:67
  289.5 7.9 %bitcast_convert_fusion = bf16[2,384,2048]{2,1,0:T(8,128)(2,1)} fusion(bf16[8,2,72,2048]{3,2,1,0:T(8,128)(2,1)} %bitcast.5, f32[8,2,72]{2,0,1:T(8,128)S(1)} %copy.53, f32[2,8,72,384]{3,2,1,0:T(8,128)} %fusion.4, f32[2,8,72,384]{3,2,1,0:T(8,128)} %fusion.2), kind=kOutput, calls=%fused_computation.8 | convolution fusion | flops 1816608768 | bytes 11407872 | tf_op jit(solution)/shard_map/slcf,slcd->lfd/dot_general | solution.py:87
  297.4 0.3 reduce-scatter.6.cloned.1.call-start
  297.6 8.4 %fusion.25 = (bf16[8,2,72]{2,0,1:T(8,128)(2,1)S(1)}, bf16[8,2,72,384]{3,2,0,1:T(8,128)(2,1)}, bf16[8,2,72,384]{3,2,0,1:T(8,128)(2,1)S(1)}) fusion(f32[2,8,72,384]{3,2,1,0:T(8,128)} %fusion.4, f32[2,8,72,384]{3,2,1,0:T(8,128)} %fusion.2, f32[8,2,72]{2,0,1:T(8,128)S(1)} %copy.53, bf16[2,384,2048]{2,1,0:T(8,128)(2,1)} %param.15, ...), kind=kOutput, calls=%fused_computation.44 | convolution fusion | flops 1819458432 | bytes 13179648 | tf_op jit(solution)/shard_map/slcd,lfd->slcf/dot_general | solution.py:78
  306.1 0.9 copy-done.4
  307.0 7.2 %bitcast_convert_fusion.1 = bf16[2,2048,384]{2,1,0:T(8,128)(2,1)} fusion(bf16[8,2,72,2048]{3,2,1,0:T(8,128)(2,1)} %bitcast.146, bf16[8,2,72,384]{3,2,0,1:T(8,128)(2,1)S(1)} %get-tuple-element.35), kind=kOutput, calls=%fused_computation.9 | convolution fusion | flops 1813512192 | bytes 8749056 | tf_op jit(solution)/shard_map/slcd,slcf->ldf/dot_general | solution.py:111
  314.2 0.3 reduce-scatter.4.cloned.1.call-start
  314.6 7.5 %bitcast_convert_fusion.2 = bf16[2,2048,384]{2,1,0:T(8,128)(2,1)} fusion(bf16[8,2,72,2048]{3,2,1,0:T(8,128)(2,1)} %bitcast.147, bf16[8,2,72,384]{3,2,0,1:T(8,128)(2,1)} %get-tuple-element.26), kind=kOutput, calls=%fused_computation.10 | convolution fusion | flops 1813512192 | bytes 8749056 | tf_op jit(solution)/shard_map/slcd,slcf->ldf/dot_general | solution.py:108
  322.1 4.0 fusion.12
  326.1 4.1 fusion
  330.3 0.6 copy.57
  330.8 2.2 dynamic-slice_bitcast_fusion
  333.1 0.7 convert_element_type.76
  333.8 3.6 all-to-all-start.3
  337.4 0.1 reduce_sum.35
  337.5 3.3 collective-permute-start.6
  340.8 0.7 collective-permute-start.5
  341.5 0.1 collective-permute-start.4
  341.6 3.3 collective-permute-start.1
  344.9 0.1 reshape.180
  345.0 6.8 %gather_fusion.3 = bf16[1024]{0:T(1024)(128)(2,1)S(1)} fusion(bf16[1152]{0:T(1024)(128)(2,1)S(1)} %reshape.180, s32[1024]{0:T(1024)S(1)} %broadcast_clamp_fusion), kind=kCustom, calls=%fused_computation.5 | custom fusion | bytes 8192 | tf_op jit(solution)/shard_map/jit(_take)/gather | solution.py:107
  351.8 0.1 gather.27
  352.0 0.7 copy.63
  352.6 0.1 collective-permute-start.2
  352.7 1.9 bitcast_dynamic-update-slice_fusion.6
  354.6 38.2 %collective-permute-done.1 = bf16[1,144,2048]{2,1,0:T(8,128)(2,1)} collective-permute-done((bf16[1,144,2048]{2,1,0:T(8,128)(2,1)}, bf16[1,144,2048]{2,1,0:T(8,128)(2,1)}, u32[]{:S(2)}, u32[]{:S(2)}) %collective-permute-start.1) | collective-permute-done | bytes 589856 | tf_op jit(solution)/shard_map/ppermute | solution.py:24
  392.8 1.6 collective-permute-start.3
  394.4 2.1 bitcast_dynamic-update-slice_fusion.5
  396.6 8.9 %collective-permute-done.2 = bf16[1,144,2048]{2,1,0:T(8,128)(2,1)S(1)} collective-permute-done((bf16[1,144,2048]{2,1,0:T(8,128)(2,1)}, bf16[1,144,2048]{2,1,0:T(8,128)(2,1)S(1)}, u32[]{:S(2)}, u32[]{:S(2)}) %collective-permute-start.2) | collective-permute-done | bytes 589856 | tf_op jit(solution)/shard_map/ppermute | solution.py:24
  405.5 0.9 bitcast_dynamic-update-slice_fusion.4
  406.4 36.7 %collective-permute-done.3 = bf16[1,144,2048]{2,1,0:T(8,128)(2,1)S(1)} collective-permute-done((bf16[1,144,2048]{2,1,0:T(8,128)(2,1)}, bf16[1,144,2048]{2,1,0:T(8,128)(2,1)S(1)}, u32[]{:S(2)}, u32[]{:S(2)}) %collective-permute-start.3) | collective-permute-done | bytes 589856 | tf_op jit(solution)/shard_map/ppermute | solution.py:24
  443.1 0.9 bitcast_dynamic-update-slice_fusion.3
  443.9 1.9 bitcast_dynamic-update-slice_fusion.2
  445.9 1.9 bitcast_dynamic-update-slice_fusion.1
  447.8 1.9 bitcast_dynamic-update-slice_fusion
  449.7 5.3 %gather_fusion.1 = bf16[8,144,2048]{2,1,0:T(8,128)(2,1)} fusion(bf16[8,144,2048]{2,1,0:T(8,128)(2,1)} %bitcast.144, s32[1024]{0:T(1024)S(1)} %pad_clamp_fusion.2), kind=kCustom, calls=%fused_computation.3 | custom fusion | bytes 9437216 | tf_op jit(solution)/shard_map/gather | solution.py:25
  455.1 11.8 %gather_fusion.2 = bf16[1024,2048]{1,0:T(8,128)(2,1)} fusion(bf16[1152,2048]{1,0:T(8,128)(2,1)} %bitcast.140, s32[1024]{0:T(1024)S(1)} %broadcast_clamp_fusion), kind=kCustom, calls=%fused_computation.4 | custom fusion | bytes 8392704 | tf_op jit(solution)/shard_map/jit(_take)/gather | solution.py:104
  466.8 5.1 %fusion.1 = bf16[128,2048]{1,0:T(8,128)(2,1)} fusion(bf16[1024,2048]{1,0:T(8,128)(2,1)} %gather_fusion.2, pred[128,8]{1,0:T(8,128)(4,1)S(1)} %get-tuple-element.22), kind=kLoop, calls=%fused_computation.15 | loop fusion | flops 3932160 | bytes 4719616 | tf_op jit(solution)/shard_map/reduce_sum | solution.py:106
  (42 shorter events, 0.3 us)
Async XLA Ops:
  7.2 177.4 %copy-start = (bf16[2,2048,384]{2,1,0:T(8,128)(2,1)S(1)}, bf16[2,2048,384]{2,1,0:T(8,128)(2,1)}, u32[]{:S(2)}) copy-start(bf16[2,2048,384]{2,1,0:T(8,128)(2,1)} %param.13) | copy-start | bytes 9437188
  26.7 42.4 %all-to-all-start = ((bf16[8,1,144]{2,1,0:T(2,128)(2,1)}), bf16[8,1,144]{2,1,0:T(2,128)(2,1)S(1)}, u32[]{:S(2)}, u32[]{:S(2)}) async-start(bf16[8,1,144]{2,1,0:T(2,128)(2,1)} %select_n.118), calls=%async_computation | async-start | bytes 16384 | tf_op jit(solution)/shard_map/all_to_all | solution.py:68
  179.6 109.9 %all-to-all-start.1 = ((bf16[8,144,2048]{2,1,0:T(8,128)(2,1)}), bf16[8,144,2048]{2,1,0:T(8,128)(2,1)}, u32[]{:S(2)}, u32[]{:S(2)}) async-start(bf16[8,144,2048]{2,1,0:T(8,128)(2,1)} %bitcast.141), calls=%async_computation.1 | async-start | bytes 9437184 | tf_op jit(solution)/shard_map/all_to_all | solution.py:67
  184.2 287.8 %reduce-scatter.8.cloned.1.call-start = ((), (), s32[]{:S(2)}) async-start(), calls=%async_computation.9 | async-start | bytes 4718592 | tf_op jit(solution)/shard_map/reduce_scatter | solution.py:117
  184.6 6.3 %copy-start.1 = (bf16[8,144,2048]{2,1,0:T(8,128)(2,1)S(1)}, bf16[8,144,2048]{2,1,0:T(8,128)(2,1)}, u32[]{:S(2)}) copy-start(bf16[8,144,2048]{2,1,0:T(8,128)(2,1)} %all_to_all.22) | copy-start | bytes 14155780
  184.6 6.3 %copy-start.2 = (bf16[2,2048,384]{2,1,0:T(8,128)(2,1)S(1)}, bf16[2,2048,384]{2,1,0:T(8,128)(2,1)}, u32[]{:S(2)}) copy-start(bf16[2,2048,384]{2,1,0:T(8,128)(2,1)} %param.14) | copy-start | bytes 9437188
  297.4 174.6 %reduce-scatter.6.cloned.1.call-start = ((), (), s32[]{:S(2)}) async-start(), calls=%async_computation.8 | async-start | bytes 4718592 | tf_op jit(solution)/shard_map/reduce_scatter | solution.py:116
  306.1 0.9 copy-start.4
  314.2 157.8 %reduce-scatter.4.cloned.1.call-start = ((), (), s32[]{:S(2)}) async-start(), calls=%async_computation.7 | async-start | bytes 4718592 | tf_op jit(solution)/shard_map/reduce_scatter | solution.py:115
  322.1 4.0 copy-start.3
  333.1 19.5 %collective-permute-start = (bf16[1,144,2048]{2,1,0:T(8,128)(2,1)}, bf16[1,144,2048]{2,1,0:T(8,128)(2,1)}, u32[]{:S(2)}, u32[]{:S(2)}) collective-permute-start(bf16[1,144,2048]{2,1,0:T(8,128)(2,1)} %get-tuple-element.33), channel_id=1, source_target_pairs={{0,2},{2,0},{4,6},{6,4},{8,10},{10,8},{12,14},{14,12},{1,3},{3,1},... | collective-permute-start | bytes 1769480 | tf_op jit(solution)/shard_map/ppermute | solution.py:24
  333.8 11.1 %all-to-all-start.3 = ((bf16[8,1,144]{2,1,0:T(2,128)(2,1)}), bf16[8,1,144]{2,1,0:T(2,128)(2,1)S(1)}, u32[]{:S(2)}, u32[]{:S(2)}) async-start(bf16[8,1,144]{2,1,0:T(2,128)(2,1)} %convert_element_type.76), calls=%async_computation.3 | async-start | bytes 16384 | tf_op jit(solution)/shard_map/all_to_all | solution.py:96
  337.5 110.3 %collective-permute-start.6 = (bf16[1,144,2048]{2,1,0:T(8,128)(2,1)}, bf16[1,144,2048]{2,1,0:T(8,128)(2,1)}, u32[]{:S(2)}, u32[]{:S(2)}) collective-permute-start(bf16[1,144,2048]{2,1,0:T(8,128)(2,1)} %get-tuple-element.27), channel_id=1, source_target_pairs={{0,14},{2,12},{4,10},{6,8},{8,6},{10,4},{12,2},{14,0},{1,15},{3,13... | collective-permute-start | bytes 1769480 | tf_op jit(solution)/shard_map/ppermute | solution.py:24
  340.8 105.1 %collective-permute-start.5 = (bf16[1,144,2048]{2,1,0:T(8,128)(2,1)}, bf16[1,144,2048]{2,1,0:T(8,128)(2,1)}, u32[]{:S(2)}, u32[]{:S(2)}) collective-permute-start(bf16[1,144,2048]{2,1,0:T(8,128)(2,1)} %get-tuple-element.28), channel_id=1, source_target_pairs={{0,12},{2,14},{4,8},{6,10},{8,4},{10,6},{12,0},{14,2},{1,13},{3,15... | collective-permute-start | bytes 1769480 | tf_op jit(solution)/shard_map/ppermute | solution.py:24
  341.5 102.5 %collective-permute-start.4 = (bf16[1,144,2048]{2,1,0:T(8,128)(2,1)}, bf16[1,144,2048]{2,1,0:T(8,128)(2,1)}, u32[]{:S(2)}, u32[]{:S(2)}) collective-permute-start(bf16[1,144,2048]{2,1,0:T(8,128)(2,1)} %get-tuple-element.29), channel_id=1, source_target_pairs={{0,10},{2,8},{4,14},{6,12},{8,2},{10,0},{12,6},{14,4},{1,11},{3,9}... | collective-permute-start | bytes 1769480 | tf_op jit(solution)/shard_map/ppermute | solution.py:24
  341.6 51.2 %collective-permute-start.1 = (bf16[1,144,2048]{2,1,0:T(8,128)(2,1)}, bf16[1,144,2048]{2,1,0:T(8,128)(2,1)}, u32[]{:S(2)}, u32[]{:S(2)}) collective-permute-start(bf16[1,144,2048]{2,1,0:T(8,128)(2,1)} %get-tuple-element.32), channel_id=1, source_target_pairs={{0,4},{2,6},{4,0},{6,2},{8,12},{10,14},{12,8},{14,10},{1,5},{3,7},... | collective-permute-start | bytes 1769480 | tf_op jit(solution)/shard_map/ppermute | solution.py:24
  352.6 52.9 %collective-permute-start.2 = (bf16[1,144,2048]{2,1,0:T(8,128)(2,1)}, bf16[1,144,2048]{2,1,0:T(8,128)(2,1)S(1)}, u32[]{:S(2)}, u32[]{:S(2)}) collective-permute-start(bf16[1,144,2048]{2,1,0:T(8,128)(2,1)} %get-tuple-element.31), channel_id=1, source_target_pairs={{0,6},{2,4},{4,2},{6,0},{8,14},{10,12},{12,10},{14,8},{1,7},{3,5},... | collective-permute-start | bytes 1769480 | tf_op jit(solution)/shard_map/ppermute | solution.py:24
  392.8 50.2 %collective-permute-start.3 = (bf16[1,144,2048]{2,1,0:T(8,128)(2,1)}, bf16[1,144,2048]{2,1,0:T(8,128)(2,1)S(1)}, u32[]{:S(2)}, u32[]{:S(2)}) collective-permute-start(bf16[1,144,2048]{2,1,0:T(8,128)(2,1)} %get-tuple-element.30), channel_id=1, source_target_pairs={{0,8},{2,10},{4,12},{6,14},{8,0},{10,2},{12,4},{14,6},{1,9},{3,11}... | collective-permute-start | bytes 1769480 | tf_op jit(solution)/shard_map/ppermute | solution.py:24
Sparse Core Ops, SparseCore 0:
  297.5 42.2 reduce-scatter.7
  342.7 43.3 reduce-scatter.5
  388.9 43.3 reduce-scatter.3
